TPU v7x, 512 devices: a whole 4x8x8 slice. The times are simulated.
512 devices in a mesh: dp: 64 (over x, y, core), ctx: 8 (over z).
Axes of the slice: x: 4, y: 8, z: 8, core: 2. Of those that a mesh axis runs over, the one named last changes fastest.
Arguments:
- queries: bfloat16 [64, 1152, 2560], P('dp', 'ctx'), may hold values from -128 to 128
- keys: bfloat16 [64, 1152, 2560], P('dp', 'ctx'), may hold values from -6 to 6
- values: bfloat16 [64, 1152, 2560], P('dp', 'ctx'), may hold values from -6 to 6
- frame_ids: int32 [64, 1152], P('dp', 'ctx'), may hold values from 0 to 15, never falling along the last dimension, each value on 1 to 144 neighbouring positions
- out_grad: bfloat16 [64, 1152, 2560], P('dp', 'ctx'), may hold values from -6 to 6
- q_prev: bfloat16 [32, 2560], replicated, may hold values from -0.125 to 0.125
- error: bfloat16 [64, 2560, 2560], P('dp', 'ctx'), may hold values from -18 to 18
Outputs:
- basis: float32 [32, 2560], P(None, 'ctx')
- q_factor: float32 [32, 2560], replicated
Inputs may be any that keep to these rules, and one draw needn't show every extreme that they name: `frame_ids`: frame numbers never fall along a clip; a frame holds at most 144 tokens.
All inputs are finite; a program needn't handle non-finite values.
Results may differ from a plain program's by a relative error of at most 0.015.
Values may be sent and summed in bfloat16 or wider, within the bound.
A program may use at most 128 MiB of HBM per device.

v0:
```python
import math

import jax
import jax.numpy as jnp
from jax import lax
from jax.sharding import PartitionSpec as P

HEADS = 20
HEAD_DIM = 128
HD = 2560


def partial_attention(query_heads, query_frames, key_piece, value_piece, frame_piece):
    count = key_piece.shape[0]
    key_heads = key_piece.reshape(count, HEADS, HEAD_DIM)
    value_heads = value_piece.reshape(count, HEADS, HEAD_DIM)
    scores = jnp.einsum(
        "thd,nhd->htn", query_heads, key_heads, preferred_element_type=jnp.float32
    ) / math.sqrt(HEAD_DIM)
    allowed = (frame_piece[None, :] <= query_frames[:, None])[None]
    scores = jnp.where(allowed, scores, jnp.float32(-1e30))
    return (scores, allowed, value_heads)


def body(queries, keys, values, frame_ids, out_grad, q_prev, error):
    tokens = queries.shape[1]
    width = queries.shape[2]
    query_heads = queries[0].reshape(tokens, HEADS, HEAD_DIM)
    own_frames = frame_ids[0]
    best = jnp.full((HEADS, tokens), -1e30, jnp.float32)
    key_piece = lax.all_gather(keys, "ctx", axis=1, tiled=True)
    value_piece = lax.all_gather(values, "ctx", axis=1, tiled=True)
    frame_piece = lax.all_gather(frame_ids, "ctx", axis=1, tiled=True)
    scores, allowed, value_heads = partial_attention(
        query_heads, own_frames, key_piece[0], value_piece[0], frame_piece[0]
    )
    fresh = jnp.maximum(best, jnp.max(scores, axis=-1))
    expo = jnp.where(allowed, jnp.exp(scores - fresh[..., None]), jnp.float32(0.0))
    total = jnp.sum(expo, axis=-1)
    update = jnp.einsum(
        "htn,nhd->htd", expo.astype(jnp.bfloat16), value_heads, preferred_element_type=jnp.float32
    )
    accum = update
    best, total, accum = (fresh, total, accum)
    mixed = accum / total[..., None]
    attn = mixed.transpose(1, 0, 2).reshape(tokens, width).astype(jnp.bfloat16)
    grad_rows = out_grad[0]
    error_rows = error[0]
    dy_proj = lax.dot_general(
        q_prev, grad_rows, (((1,), (1,)), ((), ())), preferred_element_type=jnp.float32
    ).astype(jnp.bfloat16)
    token_part = jnp.dot(dy_proj, attn, preferred_element_type=jnp.float32)
    memory_part = lax.dot_general(
        q_prev, error_rows, (((1,), (1,)), ((), ())), preferred_element_type=jnp.float32
    )
    own_share = lax.psum_scatter(
        token_part.astype(jnp.bfloat16), "ctx", scatter_dimension=1, tiled=True
    ).astype(jnp.float32)
    p_local = lax.psum(own_share + memory_part, "dp")
    gram_local = jnp.dot(p_local, p_local.T, precision=lax.Precision.HIGHEST)
    gram_matrix = lax.psum(gram_local, "ctx")
    lower = jnp.linalg.cholesky(gram_matrix)
    unit_local = jax.scipy.linalg.solve_triangular(lower, p_local, lower=True)
    unit_bf_local = unit_local.astype(jnp.bfloat16)
    unit_bf_full = lax.all_gather(unit_bf_local, "ctx", axis=1, tiled=True)
    basis = unit_local * math.sqrt(HD)
    a_proj = lax.dot_general(
        unit_bf_full, attn, (((1,), (1,)), ((), ())), preferred_element_type=jnp.float32
    ).astype(jnp.bfloat16)
    right_part = jnp.dot(a_proj, grad_rows, preferred_element_type=jnp.float32)
    right_part = right_part + jnp.dot(unit_bf_local, error_rows, preferred_element_type=jnp.float32)
    q_factor = lax.psum(right_part, ("dp", "ctx")) / lax.axis_size("dp")
    return (basis, q_factor)


def solution(mesh):
    placed = (
        P("dp", "ctx", None),
        P("dp", "ctx", None),
        P("dp", "ctx", None),
        P("dp", "ctx"),
        P("dp", "ctx", None),
        P(),
        P("dp", "ctx", None),
    )
    return jax.shard_map(
        body, mesh=mesh, in_specs=placed, out_specs=(P(None, "ctx"), P()), check_vma=False
    )
```

profile of v0, /device:TPU:1, one launch (start us, length us, event | category | flops | bytes accessed | tf_op | source)
XLA Modules:
  0.0 806.5 jit_solution(12722822576697756926)
XLA Ops:
  8.7 1.5 reshape_squeeze.9
  10.3 1.3 dynamic-slice
  12.2 0.9 dynamic-update-slice.3
  13.1 16.9 %all-reduce = s32[1152]{0:T(1024)S(1)} all-reduce(s32[1152]{0:T(1024)S(1)} %dynamic-update-slice.3), channel_id=1, replica_groups=mesh['dp'=64,'ctx'=8] {'ctx'}, use_global_device_ids=true, to_apply=%add | all-reduce | flops 1152 | bytes 9216
  30.9 59.0 %all-gather.4.cloned.1.call-done = bf16[1,1152,2560]{2,1,0:T(8,128)(2,1)} async-done(((bf16[1,144,2560]{2,1,0:T(8,128)(2,1)}), bf16[1,1152,2560]{2,1,0:T(8,128)(2,1)}) %all-gather.4.cloned.1.call-update) | async-done | bytes 5898256 | tf_op jit(solution)/shard_map/all_gather | solution.py:31
  89.8 8.8 %copy.21 = bf16[1,1152,2560]{1,2,0:T(8,128)(2,1)} copy(bf16[1,1152,2560]{2,1,0:T(8,128)(2,1)} %all-gather.4.cloned.1.call-done) | data formatting | bytes 11796480 | tf_op jit(solution)/shard_map/all_gather | solution.py:31
  98.7 5.0 fusion
  103.7 4.7 copy-done.1
  108.4 4.5 fusion.1
  112.9 51.4 %all-gather.6.cloned.1.call-done = bf16[1,1152,2560]{2,1,0:T(8,128)(2,1)} async-done(((bf16[1,144,2560]{2,1,0:T(8,128)(2,1)}), bf16[1,1152,2560]{2,1,0:T(8,128)(2,1)}) %all-gather.6.cloned.1.call-update) | async-done | bytes 5898256 | tf_op jit(solution)/shard_map/all_gather | solution.py:32
  164.3 8.9 %copy.24 = bf16[1,1152,2560]{1,2,0:T(8,128)(2,1)} copy(bf16[1,1152,2560]{2,1,0:T(8,128)(2,1)} %all-gather.6.cloned.1.call-done) | data formatting | bytes 11796480 | tf_op jit(solution)/shard_map/all_gather | solution.py:32
  173.1 10.9 %fusion.12 = bf16[20,18,8,128]{3,2,1,0:T(8,128)(2,1)S(1)} fusion(bf16[1152,20,128]{0,2,1:T(8,128)(2,1)} %bitcast.58, f32[20,144,1152]{2,1,0:T(8,128)} %copy-done.1, f32[20,144]{1,0:T(8,128)S(1)} %broadcast_maximum_fusion, pred[144,1152]{1,0:T(8,128)(4,1)S(1)} %broadcast_compare_fusion, f32[144,20]{0,1:T(8,128)S(1)} %bitcast.61), kind=kOutput, calls=%fused_computation.14 | convolution fusion | flops 866672640 | bytes 20095488 | tf_op jit(solution)/shard_map/htn,nhd->htd/dot_general | solution.py:40
  184.8 1.1 copy.33
  185.9 34.4 %reduce-scatter.4.cloned.1.call-done = bf16[320,32]{1,0:T(8,128)(2,1)} async-done(((bf16[2560,32]{1,0:T(8,128)(2,1)}), bf16[320,32]{1,0:T(8,128)(2,1)}) %reduce-scatter.4.cloned.1.call-update) | async-done | bytes 20496
  220.3 1.0 copy.34
  221.9 246.0 %psum.21 = f32[32,320]{1,0:T(8,128)S(1)} all-reduce(f32[32,320]{1,0:T(8,128)S(1)} %fusion.15), channel_id=1, replica_groups=mesh['dp'=64,'ctx'=8] {'dp'}, use_global_device_ids=true, to_apply=%region_3.4 | all-reduce | flops 10240 | bytes 81920 | tf_op jit(solution)/shard_map/psum | solution.py:59
  468.1 21.1 %psum.22 = f32[32,32]{0,1:T(8,128)S(1)} all-reduce(f32[32,32]{0,1:T(8,128)S(1)} %fusion.38), channel_id=1, replica_groups=mesh['dp'=64,'ctx'=8] {'ctx'}, use_global_device_ids=true, to_apply=%region_4.5 | all-reduce | flops 1024 | bytes 8192 | tf_op jit(solution)/shard_map/psum | solution.py:61
  489.2 2.9 cholesky.16
  493.5 2.4 custom-call.7
  496.8 18.7 %all-gather = bf16[8,320,32]{1,2,0:T(8,128)(2,1)S(1)} all-gather(bf16[1,320,32]{1,2,0:T(8,128)(2,1)S(1)} %get-tuple-element.2), channel_id=1, replica_groups=mesh['dp'=64,'ctx'=8] {'ctx'}, dimensions={0}, use_global_device_ids=true | all-gather | bytes 184320 | tf_op jit(solution)/shard_map/all_gather | solution.py:65
  516.4 1.6 fusion.18
  518.0 1.1 convolution_add_fusion
  519.2 279.1 %all-reduce.3.cloned.1.call-done = f32[32,2560]{1,0:T(8,128)} async-done(((f32[32,2560]{1,0:T(8,128)}), f32[32,2560]{1,0:T(8,128)}) %all-reduce.3.cloned.1.call-update) | async-done | bytes 327696 | tf_op jit(solution)/shard_map/psum | solution.py:72
  798.3 1.7 broadcast_multiply_fusion
  (30 shorter events, 7.1 us)
Async XLA Ops:
  7.2 214.1 %copy-start = (bf16[1,320,2560]{2,1,0:T(8,128)(2,1)S(1)}, bf16[1,320,2560]{2,1,0:T(8,128)(2,1)}, u32[]{:S(2)}) copy-start(bf16[1,320,2560]{2,1,0:T(8,128)(2,1)} %param.13) | copy-start | bytes 4915204
  7.2 82.7 %all-gather.4.cloned.1.call-start = ((), (), s32[]{:S(2)}) async-start(), calls=%async_computation.1 | async-start | bytes 6635520 | tf_op jit(solution)/shard_map/all_gather | solution.py:31
  7.9 156.3 %all-gather.6.cloned.1.call-start = ((), (), s32[]{:S(2)}) async-start(), calls=%async_computation.2 | async-start | bytes 6635520 | tf_op jit(solution)/shard_map/all_gather | solution.py:32
  8.7 211.6 %reduce-scatter.4.cloned.1.call-start = ((), (), s32[]{:S(2)}) async-start(), calls=%async_computation.4 | async-start | bytes 737280
  103.7 4.7 copy-start.1
  173.1 10.9 %copy-start.2 = (bf16[1,144,2560]{2,1,0:T(8,128)(2,1)S(1)}, bf16[1,144,2560]{2,1,0:T(8,128)(2,1)}, u32[]{:S(2)}) copy-start(bf16[1,144,2560]{2,1,0:T(8,128)(2,1)} %param.11) | copy-start | bytes 2211844
  173.1 10.9 %copy-start.3 = (bf16[32,2560]{1,0:T(8,128)(2,1)S(1)}, bf16[32,2560]{1,0:T(8,128)(2,1)}, u32[]{:S(2)}) copy-start(bf16[32,2560]{1,0:T(8,128)(2,1)} %param.12) | copy-start | bytes 491524
  185.9 612.4 %all-reduce.3.cloned.1.call-start = ((), (), s32[]{:S(2)}) async-start(), calls=%async_computation.3 | async-start | bytes 655360 | tf_op jit(solution)/shard_map/psum | solution.py:72
Sparse Core Ops, SparseCore 0:
  10.1 79.7 all-gather.3
  91.9 72.2 all-gather.5
  186.0 34.2 reduce-scatter.3
  519.3 278.9 all-reduce.2
where the time goes:
time: 808 us; the launch traced here: 807 us
  waiting for transfers between devices  425 us (53%)
  blocking collectives  303 us (38%)
  local copies, waits for them, and re-layouts  29.1 us (4%)
  matrix products  20.4 us (3%)
  between operations  14.6 us (2%)
  other arithmetic  14.4 us (2%)
    psum x1, waiting for transfers between devices, body(): q_factor = lax.psum(right_part, ('dp', 'ctx')) / lax.axis_size('dp')  279 us
    psum x1, blocking collectives, body(): p_local = lax.psum(own_share + memory_part, 'dp')  246 us
    all_gather x1, waiting for transfers between devices, body(): key_piece = lax.all_gather(keys, 'ctx', axis=1, tiled=True)  59 us
    all_gather x1, waiting for transfers between devices, body(): value_piece = lax.all_gather(values, 'ctx', axis=1, tiled=True)  51.4 us
    unnamed x5, waiting for transfers between devices  35.8 us
    psum x1, blocking collectives, body(): gram_matrix = lax.psum(gram_local, 'ctx')  21.1 us
    all_gather x1, blocking collectives, body(): unit_bf_full = lax.all_gather(unit_bf_local, 'ctx', axis=1, tiled=True)  18.7 us
    unnamed x1, blocking collectives  16.9 us
  transfers between devices with their start and end apart: 4, of which 4 were waited for; matrix products, arithmetic and copies ran while one was open for 3% of the time, Pallas kernels for 0%

commit v1 on v0

v1 whole, which is shorter than its diff:
```python
import functools
import math

import jax
import jax.numpy as jnp
from jax import lax
from jax.experimental import pallas as pl
from jax.experimental.pallas import tpu as pltpu
from jax.sharding import PartitionSpec as P

MESH = pl.DeviceIdType.MESH
F32, BF16 = jnp.float32, jnp.bfloat16
HD = 2560
TOK = 144
SEQ = 1152
NZ, NX, NY = 8, 4, 8
DEPTH = 128
ROWS = 320
BLOCK = 384
EXACT = lax.Precision.HIGHEST
SCALE = math.log2(math.e) / math.sqrt(DEPTH)
SPANS = ((0, 640), (384, 1024), (768, 1152))


def rows_by_rows(left, right, precision=None):
    return lax.dot_general(
        left, right, (((1,), (1,)), ((), ())), preferred_element_type=F32, precision=precision
    )


def kernel(
    q_in, k_in, v_in, fr_in, og_in, qp_in, er_in,
    basis, q_out,
    qkv, code, frames, dys, probs, attn, og, qp, er, mem, tok,
    cores, others, xs, ys, halves, psum, mfull, gram, grams, bsum, bs,
    part, send, got, cores2, xs2, ys2, parts,
    in_sem, recv, sent, step_recv, step_sent, tail_recv, tail_sent,
):
    dp, z = lax.axis_index("dp"), lax.axis_index("ctx")
    c, y, x = dp % 2, (dp // 2) % NY, dp // (2 * NY)
    zpar = z % 2
    par = (z + c) % 2
    mate = z + 1 - 2 * zpar
    ring = [(z + d) % NZ for d in range(1, NZ)]
    z_peers = [(dp, t) for t in ring]
    x_peers = [(((x + d) % NX) * 2 * NY + 2 * y + c, z) for d in range(1, NX)]
    y_peers = [(x * 2 * NY + 2 * ((y + d) % NY) + c, z) for d in range(1, NY)]
    core_peer = (dp + 1 - 2 * c, z)
    cross_peer = (dp + 1 - 2 * c, mate)

    def remote(src, dst, ssem, rsem, to):
        return pltpu.make_async_remote_copy(
            src_ref=src, dst_ref=dst, send_sem=ssem, recv_sem=rsem, device_id=to, device_id_type=MESH
        )

    def drain(ref, sem):
        pltpu.make_async_copy(ref, ref, sem).wait()

    loads = [
        pltpu.make_async_copy(src, dst, in_sem.at[i])
        for i, (src, dst) in enumerate(((og_in, og), (qp_in, qp), (er_in, er)))
    ]
    for load in loads:
        load.start()

    everyone = z_peers + x_peers + y_peers + [core_peer, cross_peer]
    barrier = pltpu.get_barrier_semaphore()
    for to in everyone:
        pl.semaphore_signal(barrier, inc=1, device_id=to, device_id_type=MESH)
    pl.semaphore_wait(barrier, len(everyone))

    own_rows = pl.ds(pl.multiple_of(z * TOK, 16), TOK)
    tensors = (k_in, q_in, v_in)

    def columns(slot, t):
        head = 5 * (t // 2) + (2 if slot == 0 else 3 * (t % 2) + slot - 1)
        return pl.ds(pl.multiple_of(head * DEPTH, DEPTH), DEPTH)

    def send_head(slot, steps):
        for i, src in enumerate(tensors):
            for d in steps:
                t = (z + d) % NZ
                source, target = src.at[:, columns(slot, t)], qkv.at[slot, i, own_rows]
                if d == 0:
                    pltpu.make_async_copy(source, target, recv.at[slot, i]).start()
                else:
                    remote(source, target, sent.at[slot, i], recv.at[slot, i], (dp, t)).start()

    pltpu.make_async_copy(fr_in, frames.at[z], step_recv.at[0, 5]).start()
    for to in z_peers:
        remote(fr_in, frames.at[z], tail_sent.at[0], step_recv.at[0, 5], to).start()

    @pl.when(par == 0)
    def _():
        send_head(0, (4, 2, 6, 0))

    @pl.when(par == 1)
    def _():
        send_head(0, (3, 5, 1, 7))

    loads[0].wait()
    loads[1].wait()
    dys[z] = rows_by_rows(qp[...], og[...]).astype(BF16)
    for to in z_peers:
        remote(dys.at[z], dys.at[z], tail_sent.at[1], tail_recv.at[1], to).start()
    order = (4, 3, 5, 2, 6, 1, 7, 0)
    send_head(1, order)
    send_head(2, order)

    loads[2].wait()
    head_row = pl.multiple_of(64 * zpar, 64)
    half_row = pl.multiple_of(256 * (1 - zpar), 64)
    mem[0] = jnp.zeros((32, DEPTH), F32)
    mem[0, :, 0:64] = rows_by_rows(qp[...], er[pl.ds(half_row, 64), :])
    for s in (1, 2):
        rows = pl.ds(pl.multiple_of(head_row + DEPTH * (s - 1), 64), DEPTH)
        mem[s] = rows_by_rows(qp[...], er[rows, :])
    tok[...] = jnp.zeros_like(tok)
    bsum[...] = jnp.zeros_like(bsum)
    gram[...] = jnp.zeros_like(gram)

    drain(frames, step_recv.at[0, 5])
    number = lax.broadcasted_iota(jnp.int32, (16, TOK), 0)
    place = (
        lax.broadcasted_iota(jnp.int32, (16, DEPTH), 0) == lax.broadcasted_iota(jnp.int32, (16, DEPTH), 1)
    ).astype(F32)
    for j in range(NZ):
        row = jnp.broadcast_to(frames[j], (16, TOK))
        for i, value in enumerate((jnp.where(row == number, 1.0, 0.0), jnp.where(row > number, -1e30, 0.0))):
            code[i, j * TOK : (j + 1) * TOK, :] = lax.dot_general(
                value, place, (((0,), (0,)), ((), ())), preferred_element_type=F32
            ).astype(BF16)
    drain(dys.at[0:7], tail_recv.at[1])

    lane = lax.broadcasted_iota(jnp.int32, (32, DEPTH), 1)

    def attend(s):
        drain(qkv.at[s, 0], recv.at[s, 0])
        drain(qkv.at[s, 1], recv.at[s, 1])
        for first, reach in SPANS:
            queries = jnp.concatenate([qkv[s, 1, first : first + BLOCK, :], code[0, first : first + BLOCK, :]], axis=1)
            keys = jnp.concatenate([qkv[s, 0, 0:reach, :], code[1, 0:reach, :]], axis=1)
            scores = rows_by_rows(queries, keys)
            top = jnp.max(scores, axis=1, keepdims=True)
            probs[first : first + BLOCK, 0:reach] = jnp.exp2((scores - top) * SCALE).astype(BF16)
        drain(qkv.at[s, 2], recv.at[s, 2])
        for first, reach in SPANS:
            values = jnp.concatenate([qkv[s, 2, 0:reach, :], jnp.ones((reach, DEPTH), BF16)], axis=1)
            mixed = jnp.dot(probs[first : first + BLOCK, 0:reach], values, preferred_element_type=F32)
            attn[s, first : first + BLOCK, :] = (mixed[:, 0:DEPTH] / mixed[:, DEPTH:]).astype(BF16)
        total = jnp.zeros((32, DEPTH), F32)
        for j in range(NZ):
            total += jnp.dot(dys[j], attn[s, j * TOK : (j + 1) * TOK, :], preferred_element_type=F32)
        tok[s] = total

    def add_b(s, rows):
        high = rows.astype(BF16)
        both = jnp.concatenate([high, (rows - high.astype(F32)).astype(BF16)], axis=0)
        for j in range(NZ):
            found = rows_by_rows(both, attn[s, j * TOK : (j + 1) * TOK, :])
            bsum[j] += found[0:32] + found[32:64]

    def head(s, carry):
        middle = s == 0

        @pl.when(jnp.logical_or(s > 0, par == 0))
        def _():
            attend(s)

        here = tok[s]
        turned = pltpu.roll(here, 64, 1)
        even = zpar == 0
        mine = jnp.where(lane < 64, jnp.where(even, here, turned), 0.0)
        cores[s, c] = mem[s] + jnp.where(middle, mine, here)

        @pl.when(jnp.logical_and(middle, par == 0))
        def _():
            others[1] = jnp.where(lane < 64, jnp.where(even, turned, here), 0.0)
            for t in (0, 1):
                remote(others.at[1], others.at[0], step_sent.at[0, 3], step_recv.at[0, 3], (dp - c + t, mate)).start()

        remote(cores.at[s, c], cores.at[s, c], step_sent.at[s, 0], step_recv.at[s, 0], core_peer).start()
        drain(cores.at[s, 0], step_recv.at[s, 0])
        xs[s, x] = cores[s, 0] + cores[s, 1]

        @pl.when(middle)
        def _():
            drain(others.at[0], step_recv.at[0, 3])
            xs[0, x] += others[0]

        for to in x_peers:
            remote(xs.at[s, x], xs.at[s, x], step_sent.at[s, 1], step_recv.at[s, 1], to).start()
        drain(xs.at[s, 0:3], step_recv.at[s, 1])
        ys[s, y] = (xs[s, 0] + xs[s, 1]) + (xs[s, 2] + xs[s, 3])
        for to in y_peers:
            remote(ys.at[s, y], ys.at[s, y], step_sent.at[s, 2], step_recv.at[s, 2], to).start()
        drain(ys.at[s, 0:7], step_recv.at[s, 2])
        rows = ys[s, 0]
        for j in range(1, NY):
            rows += ys[s, j]
        psum[s] = rows
        gram[:, 0:32] += rows_by_rows(rows, rows, EXACT)

        @pl.when(s == 2)
        def _():
            folded = gram[0:8]
            for j in range(1, 4):
                folded += pltpu.roll(gram[8 * j : 8 * j + 8], 32 * j, 1)
            grams[z] = folded
            for to in z_peers:
                remote(grams.at[z], grams.at[z], tail_sent.at[2], tail_recv.at[2], to).start()

        @pl.when(middle)
        def _():
            @pl.when(par == 1)
            def _():
                copy = remote(psum.at[0], halves, step_sent.at[0, 4], step_recv.at[0, 4], (dp, mate))
                copy.start()
                copy.wait_send()

            @pl.when(par == 0)
            def _():
                drain(halves, step_recv.at[0, 4])
                own, other = psum[0], halves[...]
                mfull[...] = jnp.where(even, own, other) + pltpu.roll(jnp.where(even, other, own), 64, 1)
                add_b(0, mfull[...])

        @pl.when(s > 0)
        def _():
            add_b(s, psum[s])

        return carry

    lax.fori_loop(0, 3, head, 0)

    for d in range(1, NZ):
        t = (z + d) % NZ
        remote(bsum.at[t], bs.at[z], tail_sent.at[3], tail_recv.at[3], (dp, t)).start()
    bs[z] = bsum[z]

    drain(grams.at[0:7], tail_recv.at[2])
    folded = grams[0]
    for j in range(1, NZ):
        folded += grams[j]
    line = lax.broadcasted_iota(jnp.int32, (32, DEPTH), 0)
    work = jnp.concatenate([folded] + [pltpu.roll(folded, DEPTH - 32 * j, 1) for j in range(1, 4)], axis=0)
    work = jnp.where(lane < 32, work, jnp.where(lane - 32 == line, 1.0, 0.0))
    for j in range(32):
        pivot = work[j : j + 1, j : j + 1]
        scale = 1.0 / jnp.sqrt(pivot)
        row = work[j : j + 1, :] * scale
        column = jnp.where(line[:, 0:1] > j, work[:, j : j + 1] * scale, 0.0)
        work = jnp.where(line == j, row, work - column * row)
    inverse = pltpu.roll(work, DEPTH - 32, 1)[:, 0:32]

    units = [jnp.dot(inverse, psum[s], preferred_element_type=F32, precision=EXACT) for s in range(3)]
    middle_unit, first_unit, second_unit = [unit * math.sqrt(HD) for unit in units]
    first_turned, second_turned = pltpu.roll(first_unit, 64, 1), pltpu.roll(second_unit, 64, 1)
    low, even = lane < 64, zpar == 0
    basis[:, 0:128] = jnp.where(even, first_unit, jnp.where(low, middle_unit, first_turned))
    basis[:, 128:256] = jnp.where(even, second_unit, jnp.where(low, first_turned, second_turned))
    basis[:, 256:384] = jnp.where(even, middle_unit, second_turned)

    wide = 640
    middle_bf, first_bf, second_bf = [unit.astype(BF16) for unit in units]
    for j in range(4):
        cols = slice(wide * j, wide * (j + 1))
        part[:, cols] = (
            jnp.dot(first_bf, er[pl.ds(head_row, DEPTH), cols], preferred_element_type=F32)
            + jnp.dot(second_bf, er[pl.ds(pl.multiple_of(head_row + DEPTH, 64), DEPTH), cols], preferred_element_type=F32)
            + jnp.dot(middle_bf[:, 0:64], er[pl.ds(half_row, 64), cols], preferred_element_type=F32)
        )

    drain(bs.at[0:7], tail_recv.at[3])
    summed = bs[0]
    for j in range(1, NZ):
        summed += bs[j]
    a_proj = jnp.dot(inverse, summed, preferred_element_type=F32, precision=EXACT).astype(BF16)
    for j in range(4):
        cols = slice(wide * j, wide * (j + 1))
        found = part[:, cols] + jnp.dot(a_proj, og[:, cols], preferred_element_type=F32)
        send[j] = found[0:16].astype(BF16)
        send[4 + j] = found[16:32].astype(BF16)

    for d in range(1, NZ):
        t = (z + d) % NZ
        remote(send.at[t], got.at[z], tail_sent.at[4], tail_recv.at[4], (dp, t)).start()
    got[z] = send[z]
    drain(got.at[0:7], tail_recv.at[4])
    total = got[0].astype(F32)
    for j in range(1, NZ):
        total += got[j].astype(F32)
    cores2[c] = total
    remote(cores2.at[c], cores2.at[c], tail_sent.at[5], tail_recv.at[5], core_peer).start()
    drain(cores2.at[0], tail_recv.at[5])
    xs2[x] = (cores2[0] + cores2[1]).astype(BF16)
    for to in x_peers:
        remote(xs2.at[x], xs2.at[x], tail_sent.at[6], tail_recv.at[6], to).start()
    drain(xs2.at[0:3], tail_recv.at[6])
    total = xs2[0].astype(F32)
    for j in range(1, NX):
        total += xs2[j].astype(F32)
    ys2[y] = total.astype(BF16)
    for to in y_peers:
        remote(ys2.at[y], ys2.at[y], tail_sent.at[7], tail_recv.at[7], to).start()
    drain(ys2.at[0:7], tail_recv.at[7])
    total = ys2[0].astype(F32)
    for j in range(1, NY):
        total += ys2[j].astype(F32)
    parts[z] = total.astype(BF16)
    for to in z_peers:
        remote(parts.at[z], parts.at[z], tail_sent.at[8], tail_recv.at[8], to).start()
    drain(parts.at[0:7], tail_recv.at[8])
    for j in range(NZ):
        r, g = j // 4, j % 4
        q_out[16 * r : 16 * r + 16, wide * g : wide * (g + 1)] = parts[j].astype(F32) * (1.0 / 64)

    for s in (1, 2):
        for i in range(3):
            drain(qkv.at[0, i, 0 : 7 * TOK], sent.at[s, i])

    @pl.when(par == 0)
    def _():
        for i in range(3):
            drain(qkv.at[0, i, 0 : 3 * TOK], sent.at[0, i])
        drain(others, step_sent.at[0, 3])

    @pl.when(par == 1)
    def _():
        for i in range(3):
            drain(qkv.at[0, i, 0 : 4 * TOK], sent.at[0, i])

    for s in range(3):
        drain(cores.at[s, 0], step_sent.at[s, 0])
        drain(xs.at[s, 0:3], step_sent.at[s, 1])
        drain(ys.at[s, 0:7], step_sent.at[s, 2])
    drain(frames.at[0:7], tail_sent.at[0])
    drain(dys.at[0:7], tail_sent.at[1])
    drain(grams.at[0:7], tail_sent.at[2])
    drain(bs.at[0:7], tail_sent.at[3])
    drain(got.at[0:7], tail_sent.at[4])
    drain(cores2.at[0], tail_sent.at[5])
    drain(xs2.at[0:3], tail_sent.at[6])
    drain(ys2.at[0:7], tail_sent.at[7])
    drain(parts.at[0:7], tail_sent.at[8])


def body(queries, keys, values, frame_ids, out_grad, q_prev, error):
    vmem, dma = pltpu.VMEM, pltpu.SemaphoreType.DMA
    basis, q_factor = pl.pallas_call(
        kernel,
        out_shape=(jax.ShapeDtypeStruct((32, 384), F32), jax.ShapeDtypeStruct((32, HD), F32)),
        in_specs=[pl.BlockSpec(memory_space=pl.ANY)] * 7,
        out_specs=(pl.BlockSpec(memory_space=vmem), pl.BlockSpec(memory_space=vmem)),
        scratch_shapes=[
            vmem((3, 3, SEQ, DEPTH), BF16),
            vmem((2, SEQ, DEPTH), BF16),
            vmem((NZ, 1, TOK), jnp.int32),
            vmem((NZ, 32, TOK), BF16),
            vmem((SEQ, SEQ), BF16),
            vmem((3, SEQ, DEPTH), BF16),
            vmem((TOK, HD), BF16),
            vmem((32, HD), BF16),
            vmem((ROWS, HD), BF16),
            vmem((3, 32, DEPTH), F32),
            vmem((3, 32, DEPTH), F32),
            vmem((3, 2, 32, DEPTH), F32),
            vmem((2, 32, DEPTH), F32),
            vmem((3, NX, 32, DEPTH), F32),
            vmem((3, NY, 32, DEPTH), F32),
            vmem((32, DEPTH), F32),
            vmem((3, 32, DEPTH), F32),
            vmem((32, DEPTH), F32),
            vmem((32, DEPTH), F32),
            vmem((NZ, 8, DEPTH), F32),
            vmem((NZ, 32, TOK), F32),
            vmem((NZ, 32, TOK), F32),
            vmem((32, HD), F32),
            vmem((NZ, 16, 640), BF16),
            vmem((NZ, 16, 640), BF16),
            vmem((2, 16, 640), F32),
            vmem((NX, 16, 640), BF16),
            vmem((NY, 16, 640), BF16),
            vmem((NZ, 16, 640), BF16),
            dma((3,)),
            dma((3, 3)),
            dma((3, 3)),
            dma((3, 6)),
            dma((3, 6)),
            dma((9,)),
            dma((9,)),
        ],
        compiler_params=pltpu.CompilerParams(
            collective_id=0, has_side_effects=True, vmem_limit_bytes=56 * 1024 * 1024
        ),
    )(queries[0], keys[0], values[0], frame_ids, out_grad[0], q_prev, error[0])
    return (basis[:, 0:ROWS], q_factor)


def solution(mesh):
    placed = (
        P("dp", "ctx", None),
        P("dp", "ctx", None),
        P("dp", "ctx", None),
        P("dp", "ctx"),
        P("dp", "ctx", None),
        P(),
        P("dp", "ctx", None),
    )
    return jax.shard_map(
        body, mesh=mesh, in_specs=placed, out_specs=(P(None, "ctx"), P()), check_vma=False
    )
```

time: 808 us -> 144 us (0.18)
  waiting for transfers between devices: 425 us -> 0 us
  blocking collectives: 303 us -> 0 us
  Pallas kernels: 0 us -> 140 us
  local copies, waits for them, and re-layouts: 29.1 us -> 3.14 us
  matrix products: 20.4 us -> 0 us
  other arithmetic: 14.4 us -> 0 us
  between operations: 14.6 us -> 0.64 us
    psum x1 -> x0, waiting for transfers between devices: 279 us -> none  [body(): q_factor = lax.psum(right_part, ('dp', 'ctx')) / lax.axis_size('dp')]
    psum x2 -> x0, blocking collectives: 267 us -> none  [the longest x1 246 us: body(): p_local = lax.psum(own_share + memory_part, 'dp')]
    pallas_call x0 -> x1, Pallas kernels: none -> 140 us  [body(): pl.pallas_call(kernel, out_shape=(jax.ShapeDtypeStruct((32, 384), F32), j...]
    all_gather x2 -> x0, waiting for transfers between devices: 110 us -> none  [the longest x1 59 us: body(): key_piece = lax.all_gather(keys, 'ctx', axis=1, tiled=True)]
    unnamed x5 -> x0, waiting for transfers between devices: 35.8 us -> none
    dot_general x7 -> x0, matrix products: 20.1 us -> none  [the longest x1 10.9 us: body(): jnp.einsum('htn,nhd->htd', expo.astype(jnp.bfloat16), value_heads, prefer...]
    all_gather x1 -> x0, blocking collectives: 18.7 us -> none  [body(): unit_bf_full = lax.all_gather(unit_bf_local, 'ctx', axis=1, tiled=True)]
    all_gather x3 -> x0, local copies, waits for them, and re-layouts: 17.7 us -> none  [the longest x1 8.86 us: body(): value_piece = lax.all_gather(values, 'ctx', axis=1, tiled=True)]
  transfers between devices with their start and end apart: 4 -> 0, of which waited for: 4 -> 0; matrix products, arithmetic and copies ran while one was open for 3% -> 0% of each run, Pallas kernels for 0% -> 0%
where the time goes in v1:
time: 144 us
  Pallas kernels  140 us (97%)
  local copies, waits for them, and re-layouts  3.14 us (2%)
    pallas_call x1, Pallas kernels, body(): pl.pallas_call(kernel, out_shape=(jax.ShapeDtypeStruct((32, 384), F32), j...  140 us
    unnamed x2, local copies, waits for them, and re-layouts  3.14 us

profile of v1, /device:TPU:1, one launch (start us, length us, event | category | flops | bytes accessed | tf_op | source)
XLA Modules:
  0.0 144.2 jit_solution(1681640540279694949)
XLA Ops:
  0.6 140.4 %shard_map.86 = (f32[32,384]{1,0:T(8,128)}, f32[32,2560]{1,0:T(8,128)}) custom-call(bf16[144,2560]{1,0:T(8,128)(2,1)} %bitcast.7, bf16[144,2560]{1,0:T(8,128)(2,1)} %bitcast.8, bf16[144,2560]{1,0:T(8,128)(2,1)} %bitcast.9, s32[1,144]{1,0:T(1,128)} %fr_in.1, bf16[144,2560]{1,0:T(8,128)(2,1)} %bitcast.10, bf16[32,2560]{1,0:T(8,128)(2,1)} %qp_in.1, ...), custom_call_target="tpu_custom_call" | custom-call | tf_op jit(solution)/shard_map/pallas_call | solution.py:350
  141.1 1.4 copy.11
  142.5 1.7 %copy.12 = f32[32,2560]{1,0:T(8,128)} copy(f32[32,2560]{1,0:T(8,128)} %get-tuple-element.9) | data formatting | bytes 655360

commit v2 on v1

v2 whole, which is shorter than its diff:
```python
import functools
import math

import jax
import jax.numpy as jnp
from jax import lax
from jax.experimental import pallas as pl
from jax.experimental.pallas import tpu as pltpu
from jax.sharding import PartitionSpec as P

MESH = pl.DeviceIdType.MESH
F32, BF16 = jnp.float32, jnp.bfloat16
HD = 2560
TOK = 144
SEQ = 1152
NZ, NX, NY = 8, 4, 8
DEPTH = 128
ROWS = 320
BLOCK = 384
EXACT = lax.Precision.HIGHEST
SCALE = math.log2(math.e) / math.sqrt(DEPTH)
SPANS = ((0, 640), (384, 1024), (768, 1152))


def rows_by_rows(left, right, precision=None):
    return lax.dot_general(
        left, right, (((1,), (1,)), ((), ())), preferred_element_type=F32, precision=precision
    )


def kernel(
    q_in, k_in, v_in, fr_in, og_in, qp_in, er_in,
    basis, q_out,
    qkv, code, frames, dys, probs, attn, og, qp, er, mem, tok,
    cores, others, xs, ys, halves, psum, gram, grams, bsum, bpack, bs,
    part, send, got, cores2, xs2, ys2,
    in_sem, recv, sent, step_recv, step_sent, tail_recv, tail_sent,
):
    dp, z = lax.axis_index("dp"), lax.axis_index("ctx")
    c, y, x = dp % 2, (dp // 2) % NY, dp // (2 * NY)
    zpar = z % 2
    par = (z + c) % 2
    mate = z + 1 - 2 * zpar
    even = zpar == 0
    far = (4, 3, 5, 2, 6, 1, 7)
    z_peers = [(dp, (z + d) % NZ) for d in far]
    x_peers = [(((x + d) % NX) * 2 * NY + 2 * y + c, z) for d in (2, 1, 3)]
    y_peers = [(x * 2 * NY + 2 * ((y + d) % NY) + c, z) for d in far]
    core_peer = (dp + 1 - 2 * c, z)
    cross_peer = (dp + 1 - 2 * c, mate)

    def remote(src, dst, ssem, rsem, to):
        return pltpu.make_async_remote_copy(
            src_ref=src, dst_ref=dst, send_sem=ssem, recv_sem=rsem, device_id=to, device_id_type=MESH
        )

    def drain(ref, sem):
        pltpu.make_async_copy(ref, ref, sem).wait()

    loads = [
        pltpu.make_async_copy(src, dst, in_sem.at[i])
        for i, (src, dst) in enumerate(((og_in, og), (qp_in, qp), (er_in, er)))
    ]
    for load in loads:
        load.start()

    everyone = z_peers + x_peers + y_peers + [core_peer, cross_peer]
    barrier = pltpu.get_barrier_semaphore()
    for to in everyone:
        pl.semaphore_signal(barrier, inc=1, device_id=to, device_id_type=MESH)
    pl.semaphore_wait(barrier, len(everyone))

    own_rows = pl.ds(pl.multiple_of(z * TOK, 16), TOK)
    tensors = (k_in, q_in, v_in)

    def columns(slot, t):
        head = 5 * (t // 2) + (2 if slot == 0 else 3 * (t % 2) + slot - 1)
        return pl.ds(pl.multiple_of(head * DEPTH, DEPTH), DEPTH)

    def send_to(slot, i, steps):
        for d in steps:
            t = (z + d) % NZ
            source, target = tensors[i].at[:, columns(slot, t)], qkv.at[slot, i, own_rows]
            if d == 0:
                pltpu.make_async_copy(source, target, recv.at[slot, i]).start()
            else:
                remote(source, target, sent.at[slot, i], recv.at[slot, i], (dp, t)).start()

    def send_head(slot, i):
        if slot > 0:
            send_to(slot, i, far + (0,))
            return

        @pl.when(par == 0)
        def _():
            send_to(0, i, (4, 2, 6, 0))

        @pl.when(par == 1)
        def _():
            send_to(0, i, (3, 5, 1, 7))

    def left(slot, i):
        if slot > 0:
            drain(qkv.at[0, i, 0 : 7 * TOK], sent.at[slot, i])
            return

        @pl.when(par == 0)
        def _():
            drain(qkv.at[0, i, 0 : 3 * TOK], sent.at[0, i])

        @pl.when(par == 1)
        def _():
            drain(qkv.at[0, i, 0 : 4 * TOK], sent.at[0, i])

    pltpu.make_async_copy(fr_in, frames.at[z], step_recv.at[5]).start()
    for to in z_peers:
        remote(fr_in, frames.at[z], tail_sent.at[0], step_recv.at[5], to).start()

    for i in range(3):
        send_head(0, i)

    loads[0].wait()
    loads[1].wait()
    dys[z] = rows_by_rows(qp[...], og[...]).astype(BF16)
    for to in z_peers:
        remote(dys.at[z], dys.at[z], tail_sent.at[1], tail_recv.at[1], to).start()
    send_head(1, 0)

    loads[2].wait()
    head_row = pl.multiple_of(64 * zpar, 64)
    half_row = pl.multiple_of(256 * (1 - zpar), 64)
    halves[...] = jnp.zeros((32, DEPTH), F32)
    halves[:, 0:64] = rows_by_rows(qp[...], er[pl.ds(half_row, 64), :])
    mine = halves[...]
    mem[0] = jnp.where(even, mine, pltpu.roll(mine, 64, 1))
    remote(mem.at[0], others.at[0], step_sent.at[4], step_recv.at[4], (dp, mate)).start()
    for s in (1, 2):
        rows = pl.ds(pl.multiple_of(head_row + DEPTH * (s - 1), 64), DEPTH)
        mem[s] = rows_by_rows(qp[...], er[rows, :])
    tok[...] = jnp.zeros_like(tok)
    bsum[...] = jnp.zeros_like(bsum)
    bpack[...] = jnp.zeros_like(bpack)
    gram[...] = jnp.zeros_like(gram)

    drain(frames, step_recv.at[5])
    number = lax.broadcasted_iota(jnp.int32, (16, TOK), 0)
    place = (
        lax.broadcasted_iota(jnp.int32, (16, DEPTH), 0) == lax.broadcasted_iota(jnp.int32, (16, DEPTH), 1)
    ).astype(F32)
    for j in range(NZ):
        row = jnp.broadcast_to(frames[j], (16, TOK))
        for i, value in enumerate((jnp.where(row == number, 1.0, 0.0), jnp.where(row > number, -1e30, 0.0))):
            code[i, j * TOK : (j + 1) * TOK, :] = lax.dot_general(
                value, place, (((0,), (0,)), ((), ())), preferred_element_type=F32
            ).astype(BF16)
    drain(dys.at[0:7], tail_recv.at[1])

    lane = lax.broadcasted_iota(jnp.int32, (32, DEPTH), 1)

    def attend(s):
        drain(qkv.at[s, 0], recv.at[s, 0])
        drain(qkv.at[s, 1], recv.at[s, 1])
        for first, reach in SPANS:
            queries = jnp.concatenate([qkv[s, 1, first : first + BLOCK, :], code[0, first : first + BLOCK, :]], axis=1)
            keys = jnp.concatenate([qkv[s, 0, 0:reach, :], code[1, 0:reach, :]], axis=1)
            scores = rows_by_rows(queries, keys)
            top = jnp.max(scores, axis=1, keepdims=True)
            probs[first : first + BLOCK, 0:reach] = jnp.exp2((scores - top) * SCALE).astype(BF16)
        drain(qkv.at[s, 2], recv.at[s, 2])
        for first, reach in SPANS:
            values = jnp.concatenate([qkv[s, 2, 0:reach, :], jnp.ones((reach, DEPTH), BF16)], axis=1)
            mixed = jnp.dot(probs[first : first + BLOCK, 0:reach], values, preferred_element_type=F32)
            attn[s, first : first + BLOCK, :] = (mixed[:, 0:DEPTH] / mixed[:, DEPTH:]).astype(BF16)
        total = jnp.zeros((32, DEPTH), F32)
        for j in range(NZ):
            total += jnp.dot(dys[j], attn[s, j * TOK : (j + 1) * TOK, :], preferred_element_type=F32)
        tok[s] = total

    def add_b(s, rows):
        high = rows.astype(BF16)
        both = jnp.concatenate([high, (rows - high.astype(F32)).astype(BF16)], axis=0)
        for j in range(NZ):
            found = rows_by_rows(both, attn[s, j * TOK : (j + 1) * TOK, :])
            bsum[j] += found[0:32] + found[32:64]

    def head(s, carry):
        @pl.when(s == 0)
        def _():
            for i, ahead in enumerate(((1, 1), (1, 2), (2, 0))):
                left(0, i)
                send_head(*ahead)

        @pl.when(s == 1)
        def _():
            for i, ahead in enumerate(((2, 1), (2, 2))):
                left(1, i)
                send_head(*ahead)

        @pl.when(jnp.logical_or(s > 0, par == 0))
        def _():
            attend(s)

        here = tok[s]
        cores[c, s] = mem[s] + here

        @pl.when(jnp.logical_and(s == 0, par == 0))
        def _():
            for t in (0, 1):
                remote(tok.at[0], others.at[1], step_sent.at[3], step_recv.at[3], (dp - c + t, mate)).start()

        return carry

    lax.fori_loop(0, 3, head, 0)

    drain(others.at[0], step_recv.at[4])
    cores[c, 0] += others[0]
    remote(cores.at[c], cores.at[c], step_sent.at[0], step_recv.at[0], core_peer).start()
    drain(others.at[1], step_recv.at[3])
    drain(cores.at[0], step_recv.at[0])
    total = cores[0] + cores[1]
    xs[x] = total.astype(BF16)
    xs[x, 0] = (total[0] + others[1]).astype(BF16)
    for to in x_peers:
        remote(xs.at[x], xs.at[x], step_sent.at[1], step_recv.at[1], to).start()
    drain(xs.at[0:3], step_recv.at[1])
    total = xs[0].astype(F32)
    for j in range(1, NX):
        total += xs[j].astype(F32)
    ys[y] = total.astype(BF16)
    for to in y_peers:
        remote(ys.at[y], ys.at[y], step_sent.at[2], step_recv.at[2], to).start()
    drain(ys.at[0:7], step_recv.at[2])
    total = ys[0].astype(F32)
    for j in range(1, NY):
        total += ys[j].astype(F32)
    psum[...] = total

    own = jnp.where((lane < 64) == even, psum[0], 0.0)
    gram[:, 0:32] = rows_by_rows(own, own, EXACT)
    for s in (1, 2):
        gram[:, 0:32] += rows_by_rows(psum[s], psum[s], EXACT)
    folded = gram[0:8]
    for j in range(1, 4):
        folded += pltpu.roll(gram[8 * j : 8 * j + 8], 32 * j, 1)
    grams[z] = folded
    for to in z_peers:
        remote(grams.at[z], grams.at[z], tail_sent.at[2], tail_recv.at[2], to).start()

    add_b(1, psum[1])
    add_b(2, psum[2])

    @pl.when(par == 0)
    def _():
        add_b(0, psum[0])

    for j in range(NZ):
        bpack[j, 0:32] = bsum[j, :, 0:DEPTH]
        for i in range(4):
            bpack[j, 32:40, 16 * i : 16 * i + 16] = bsum[j, 8 * i : 8 * i + 8, DEPTH:TOK]
    for d in far:
        t = (z + d) % NZ
        remote(bpack.at[t], bs.at[z], tail_sent.at[3], tail_recv.at[3], (dp, t)).start()
    bs[z] = bpack[z]

    drain(grams.at[0:7], tail_recv.at[2])
    folded = grams[0]
    for j in range(1, NZ):
        folded += grams[j]
    line = lax.broadcasted_iota(jnp.int32, (32, DEPTH), 0)
    work = jnp.concatenate([folded] + [pltpu.roll(folded, DEPTH - 32 * j, 1) for j in range(1, 4)], axis=0)
    work = jnp.where(lane < 32, work, jnp.where(lane - 32 == line, 1.0, 0.0))
    for j in range(32):
        pivot = work[j : j + 1, j : j + 1]
        scale = 1.0 / jnp.sqrt(pivot)
        row = work[j : j + 1, :] * scale
        column = jnp.where(line[:, 0:1] > j, work[:, j : j + 1] * scale, 0.0)
        work = jnp.where(line == j, row, work - column * row)
    inverse = pltpu.roll(work, DEPTH - 32, 1)[:, 0:32]

    units = [jnp.dot(inverse, psum[s], preferred_element_type=F32, precision=EXACT) for s in range(3)]
    middle_unit, first_unit, second_unit = [unit * math.sqrt(HD) for unit in units]
    first_turned, second_turned = pltpu.roll(first_unit, 64, 1), pltpu.roll(second_unit, 64, 1)
    low = lane < 64
    middle_turned = pltpu.roll(middle_unit, 64, 1)
    basis[:, 0:128] = jnp.where(even, first_unit, jnp.where(low, middle_turned, first_turned))
    basis[:, 128:256] = jnp.where(even, second_unit, jnp.where(low, first_turned, second_turned))
    basis[:, 256:384] = jnp.where(even, middle_unit, second_turned)

    wide = 640
    units[0] = jnp.where(even, units[0], pltpu.roll(units[0], 64, 1))
    middle_bf, first_bf, second_bf = [unit.astype(BF16) for unit in units]
    for j in range(4):
        cols = slice(wide * j, wide * (j + 1))
        part[:, cols] = (
            jnp.dot(first_bf, er[pl.ds(head_row, DEPTH), cols], preferred_element_type=F32)
            + jnp.dot(second_bf, er[pl.ds(pl.multiple_of(head_row + DEPTH, 64), DEPTH), cols], preferred_element_type=F32)
            + jnp.dot(middle_bf[:, 0:64], er[pl.ds(half_row, 64), cols], preferred_element_type=F32)
        )

    drain(bs.at[0:7], tail_recv.at[3])
    summed = bs[0]
    for j in range(1, NZ):
        summed += bs[j]
    rest = jnp.concatenate([summed[32:40, 16 * i : 16 * i + 16] for i in range(4)], axis=0)
    a_proj = jnp.dot(inverse, summed[0:32], preferred_element_type=F32, precision=EXACT).astype(BF16)
    a_rest = jnp.dot(inverse, rest, preferred_element_type=F32, precision=EXACT).astype(BF16)
    for j in range(4):
        cols = slice(wide * j, wide * (j + 1))
        found = part[:, cols] + jnp.dot(a_proj, og[0:DEPTH, cols], preferred_element_type=F32)
        found += jnp.dot(a_rest, og[DEPTH:TOK, cols], preferred_element_type=F32)
        send[j] = found[0:16].astype(BF16)
        send[4 + j] = found[16:32].astype(BF16)

    for d in far:
        t = (z + d) % NZ
        remote(send.at[t], got.at[z], tail_sent.at[4], tail_recv.at[4], (dp, t)).start()
    got[z] = send[z]
    drain(got.at[0:7], tail_recv.at[4])
    total = got[0].astype(F32)
    for j in range(1, NZ):
        total += got[j].astype(F32)
    cores2[c] = total
    remote(cores2.at[c], cores2.at[c], tail_sent.at[5], tail_recv.at[5], core_peer).start()
    drain(cores2.at[0], tail_recv.at[5])
    xs2[x] = (cores2[0] + cores2[1]).astype(BF16)
    for to in x_peers:
        remote(xs2.at[x], xs2.at[x], tail_sent.at[6], tail_recv.at[6], to).start()
    drain(xs2.at[0:3], tail_recv.at[6])
    total = xs2[0].astype(F32)
    for j in range(1, NX):
        total += xs2[j].astype(F32)
    ys2[y] = total.astype(BF16)
    for to in y_peers:
        remote(ys2.at[y], ys2.at[y], tail_sent.at[7], tail_recv.at[7], to).start()
    drain(ys2.at[0:7], tail_recv.at[7])
    total = ys2[0].astype(F32)
    for j in range(1, NY):
        total += ys2[j].astype(F32)
    q_out[z] = total.astype(BF16)
    for to in z_peers:
        remote(q_out.at[z], q_out.at[z], tail_sent.at[8], tail_recv.at[8], to).start()
    drain(q_out.at[0:7], tail_recv.at[8])
    for s, i in ((1, 2), (2, 0), (2, 1), (2, 2)):
        left(s, i)

    @pl.when(par == 0)
    def _():
        drain(others, step_sent.at[3])

    drain(mem.at[0], step_sent.at[4])
    drain(cores.at[0], step_sent.at[0])
    drain(xs.at[0:3], step_sent.at[1])
    drain(ys.at[0:7], step_sent.at[2])
    drain(frames.at[0:7], tail_sent.at[0])
    drain(dys.at[0:7], tail_sent.at[1])
    drain(grams.at[0:7], tail_sent.at[2])
    drain(bs.at[0:7], tail_sent.at[3])
    drain(got.at[0:7], tail_sent.at[4])
    drain(cores2.at[0], tail_sent.at[5])
    drain(xs2.at[0:3], tail_sent.at[6])
    drain(ys2.at[0:7], tail_sent.at[7])
    drain(q_out.at[0:7], tail_sent.at[8])


def finish(wide_basis, parts, basis, q_out):
    basis[...] = wide_basis[:, 0:ROWS]
    for j in range(NZ):
        r, g = j // 4, j % 4
        q_out[16 * r : 16 * r + 16, 640 * g : 640 * (g + 1)] = parts[j].astype(F32) * (1.0 / 64)


def body(queries, keys, values, frame_ids, out_grad, q_prev, error):
    vmem, dma = pltpu.VMEM, pltpu.SemaphoreType.DMA
    basis, q_factor = pl.pallas_call(
        kernel,
        out_shape=(jax.ShapeDtypeStruct((32, 384), F32), jax.ShapeDtypeStruct((NZ, 16, 640), BF16)),
        in_specs=[pl.BlockSpec(memory_space=pl.ANY)] * 7,
        out_specs=(pl.BlockSpec(memory_space=vmem), pl.BlockSpec(memory_space=vmem)),
        scratch_shapes=[
            vmem((3, 3, SEQ, DEPTH), BF16),
            vmem((2, SEQ, DEPTH), BF16),
            vmem((NZ, 1, TOK), jnp.int32),
            vmem((NZ, 32, TOK), BF16),
            vmem((SEQ, SEQ), BF16),
            vmem((3, SEQ, DEPTH), BF16),
            vmem((TOK, HD), BF16),
            vmem((32, HD), BF16),
            vmem((ROWS, HD), BF16),
            vmem((3, 32, DEPTH), F32),
            vmem((3, 32, DEPTH), F32),
            vmem((2, 3, 32, DEPTH), F32),
            vmem((2, 32, DEPTH), F32),
            vmem((NX, 3, 32, DEPTH), BF16),
            vmem((NY, 3, 32, DEPTH), BF16),
            vmem((32, DEPTH), F32),
            vmem((3, 32, DEPTH), F32),
            vmem((32, DEPTH), F32),
            vmem((NZ, 8, DEPTH), F32),
            vmem((NZ, 32, TOK), F32),
            vmem((NZ, 40, DEPTH), F32),
            vmem((NZ, 40, DEPTH), F32),
            vmem((32, HD), F32),
            vmem((NZ, 16, 640), BF16),
            vmem((NZ, 16, 640), BF16),
            vmem((2, 16, 640), F32),
            vmem((NX, 16, 640), BF16),
            vmem((NY, 16, 640), BF16),
            dma((3,)),
            dma((3, 3)),
            dma((3, 3)),
            dma((6,)),
            dma((6,)),
            dma((9,)),
            dma((9,)),
        ],
        compiler_params=pltpu.CompilerParams(
            collective_id=0, has_side_effects=True, vmem_limit_bytes=56 * 1024 * 1024
        ),
    )(queries[0], keys[0], values[0], frame_ids, out_grad[0], q_prev, error[0])
    return pl.pallas_call(
        finish,
        out_shape=(jax.ShapeDtypeStruct((32, ROWS), F32), jax.ShapeDtypeStruct((32, HD), F32)),
    )(basis, q_factor)


def solution(mesh):
    placed = (
        P("dp", "ctx", None),
        P("dp", "ctx", None),
        P("dp", "ctx", None),
        P("dp", "ctx"),
        P("dp", "ctx", None),
        P(),
        P("dp", "ctx", None),
    )
    return jax.shard_map(
        body, mesh=mesh, in_specs=placed, out_specs=(P(None, "ctx"), P()), check_vma=False
    )
```

time: 144 us -> 114 us (0.79)
  Pallas kernels: 140 us -> 113 us
  local copies, waits for them, and re-layouts: 3.14 us -> 0 us
    pallas_call x1, Pallas kernels: 140 us -> 112 us  [body(): pl.pallas_call(kernel, out_shape=(jax.ShapeDtypeStruct((32, 384), F32), j...]
    unnamed x2 -> x0, local copies, waits for them, and re-layouts: 3.14 us -> none
    pallas_call x0 -> x1, Pallas kernels: none -> 1.7 us  [body(): pl.pallas_call(finish, out_shape=(jax.ShapeDtypeStruct((32, ROWS), F32),...]
where the time goes in v2:
time: 114 us
  Pallas kernels  113 us (99%)
    pallas_call x1, Pallas kernels, body(): pl.pallas_call(kernel, out_shape=(jax.ShapeDtypeStruct((32, 384), F32), j...  112 us

profile of v2, /device:TPU:1, one launch (start us, length us, event | category | flops | bytes accessed | tf_op | source)
XLA Modules:
  0.0 113.9 jit_solution(1908002959345807507)
XLA Ops:
  0.6 111.5 %shard_map.86 = (f32[32,384]{1,0:T(8,128)}, bf16[8,16,640]{2,1,0:T(8,128)(2,1)}) custom-call(bf16[144,2560]{1,0:T(8,128)(2,1)} %bitcast.6, bf16[144,2560]{1,0:T(8,128)(2,1)} %bitcast.7, bf16[144,2560]{1,0:T(8,128)(2,1)} %bitcast.8, s32[1,144]{1,0:T(1,128)} %fr_in.1, bf16[144,2560]{1,0:T(8,128)(2,1)} %bitcast.9, bf16[32,2560]{1,0:T(8,128)(2,1)} %qp_in.1, ...), custom_call_target="tpu_custom_call" | custom-call | tf_op jit(solution)/shard_map/pallas_call | solution.py:374
  112.2 1.7 %shard_map.87 = (f32[32,320]{1,0:T(8,128)}, f32[32,2560]{1,0:T(8,128)}) custom-call(f32[32,384]{1,0:T(8,128)} %get-tuple-element.4.wide_basis, bf16[8,16,640]{2,1,0:T(8,128)(2,1)} %get-tuple-element.5.parts), custom_call_target="tpu_custom_call" | custom-call | tf_op jit(solution)/shard_map/pallas_call | solution.py:420

commit v3 on v2

--- a/solution.py
+++ b/solution.py
@@ -31,9 +31,9 @@
 def kernel(
     q_in, k_in, v_in, fr_in, og_in, qp_in, er_in,
     basis, q_out,
-    qkv, code, frames, dys, probs, attn, og, qp, er, mem, tok,
-    cores, others, xs, ys, halves, psum, gram, grams, bsum, bpack, bs,
-    part, send, got, cores2, xs2, ys2,
+    qkv, code, frames, dys, packed, probs, attn, og, qp, er, mem, tok,
+    others, xs, ys, halves, psum, gram, grams, bpack, bs,
+    part, send, got, ys2, zs2,
     in_sem, recv, sent, step_recv, step_sent, tail_recv, tail_sent,
 ):
     dp, z = lax.axis_index("dp"), lax.axis_index("ctx")
@@ -44,10 +44,10 @@
     even = zpar == 0
     far = (4, 3, 5, 2, 6, 1, 7)
     z_peers = [(dp, (z + d) % NZ) for d in far]
-    x_peers = [(((x + d) % NX) * 2 * NY + 2 * y + c, z) for d in (2, 1, 3)]
+    w = 2 * x + c
+    w_peers = [(((x + d) % NX) * 2 * NY + 2 * y + t, z) for d in (2, 1, 3) for t in (c, 1 - c)]
+    w_peers.append((dp + 1 - 2 * c, z))
     y_peers = [(x * 2 * NY + 2 * ((y + d) % NY) + c, z) for d in far]
-    core_peer = (dp + 1 - 2 * c, z)
-    cross_peer = (dp + 1 - 2 * c, mate)
 
     def remote(src, dst, ssem, rsem, to):
         return pltpu.make_async_remote_copy(
@@ -64,7 +64,7 @@
     for load in loads:
         load.start()
 
-    everyone = z_peers + x_peers + y_peers + [core_peer, cross_peer]
+    everyone = z_peers + w_peers + y_peers
     barrier = pltpu.get_barrier_semaphore()
     for to in everyone:
         pl.semaphore_signal(barrier, inc=1, device_id=to, device_id_type=MESH)
@@ -112,16 +112,21 @@
         def _():
             drain(qkv.at[0, i, 0 : 4 * TOK], sent.at[0, i])
 
+    send_head(0, 0)
     pltpu.make_async_copy(fr_in, frames.at[z], step_recv.at[5]).start()
     for to in z_peers:
         remote(fr_in, frames.at[z], tail_sent.at[0], step_recv.at[5], to).start()
-
-    for i in range(3):
-        send_head(0, i)
+    send_head(0, 1)
+    send_head(0, 2)
 
     loads[0].wait()
     loads[1].wait()
-    dys[z] = rows_by_rows(qp[...], og[...]).astype(BF16)
+    found = rows_by_rows(qp[...], og[...])
+    packed[...] = jnp.zeros_like(packed)
+    packed[0:32] = found[:, 0:DEPTH]
+    packed[32:48, 0:16] = found[0:16, DEPTH:]
+    packed[32:48, 16:32] = found[16:32, DEPTH:]
+    dys[z] = packed[...].astype(BF16)
     for to in z_peers:
         remote(dys.at[z], dys.at[z], tail_sent.at[1], tail_recv.at[1], to).start()
     send_head(1, 0)
@@ -138,7 +143,6 @@
         rows = pl.ds(pl.multiple_of(head_row + DEPTH * (s - 1), 64), DEPTH)
         mem[s] = rows_by_rows(qp[...], er[rows, :])
     tok[...] = jnp.zeros_like(tok)
-    bsum[...] = jnp.zeros_like(bsum)
     bpack[...] = jnp.zeros_like(bpack)
     gram[...] = jnp.zeros_like(gram)
 
@@ -173,15 +177,11 @@
             attn[s, first : first + BLOCK, :] = (mixed[:, 0:DEPTH] / mixed[:, DEPTH:]).astype(BF16)
         total = jnp.zeros((32, DEPTH), F32)
         for j in range(NZ):
-            total += jnp.dot(dys[j], attn[s, j * TOK : (j + 1) * TOK, :], preferred_element_type=F32)
+            main, rest = dys[j, 0:32, :], dys[j, 32:48, :].astype(F32)
+            rest = jnp.concatenate([rest, pltpu.roll(rest, DEPTH - 16, 1)], axis=0)[:, 0:16].astype(BF16)
+            total += jnp.dot(main, attn[s, j * TOK : j * TOK + DEPTH, :], preferred_element_type=F32)
+            total += jnp.dot(rest, attn[s, j * TOK + DEPTH : (j + 1) * TOK, :], preferred_element_type=F32)
         tok[s] = total
-
-    def add_b(s, rows):
-        high = rows.astype(BF16)
-        both = jnp.concatenate([high, (rows - high.astype(F32)).astype(BF16)], axis=0)
-        for j in range(NZ):
-            found = rows_by_rows(both, attn[s, j * TOK : (j + 1) * TOK, :])
-            bsum[j] += found[0:32] + found[32:64]
 
     def head(s, carry):
         @pl.when(s == 0)
@@ -200,31 +200,30 @@
         def _():
             attend(s)
 
-        here = tok[s]
-        cores[c, s] = mem[s] + here
-
         @pl.when(jnp.logical_and(s == 0, par == 0))
         def _():
-            for t in (0, 1):
-                remote(tok.at[0], others.at[1], step_sent.at[3], step_recv.at[3], (dp - c + t, mate)).start()
+            remote(tok.at[0], others.at[1], step_sent.at[3], step_recv.at[3], (dp, mate)).start()
 
         return carry
 
     lax.fori_loop(0, 3, head, 0)
 
     drain(others.at[0], step_recv.at[4])
-    cores[c, 0] += others[0]
-    remote(cores.at[c], cores.at[c], step_sent.at[0], step_recv.at[0], core_peer).start()
-    drain(others.at[1], step_recv.at[3])
-    drain(cores.at[0], step_recv.at[0])
-    total = cores[0] + cores[1]
-    xs[x] = total.astype(BF16)
-    xs[x, 0] = (total[0] + others[1]).astype(BF16)
-    for to in x_peers:
-        remote(xs.at[x], xs.at[x], step_sent.at[1], step_recv.at[1], to).start()
-    drain(xs.at[0:3], step_recv.at[1])
+
+    @pl.when(par == 1)
+    def _():
+        attn[0] = jnp.zeros((SEQ, DEPTH), BF16)
+        drain(others.at[1], step_recv.at[3])
+        tok[0] = others[1]
+
+    xs[w, 0] = ((mem[0] + others[0]) + tok[0]).astype(BF16)
+    xs[w, 1] = (mem[1] + tok[1]).astype(BF16)
+    xs[w, 2] = (mem[2] + tok[2]).astype(BF16)
+    for to in w_peers:
+        remote(xs.at[w], xs.at[w], step_sent.at[1], step_recv.at[1], to).start()
+    drain(xs.at[0:7], step_recv.at[1])
     total = xs[0].astype(F32)
-    for j in range(1, NX):
+    for j in range(1, 8):
         total += xs[j].astype(F32)
     ys[y] = total.astype(BF16)
     for to in y_peers:
@@ -246,21 +245,25 @@
     for to in z_peers:
         remote(grams.at[z], grams.at[z], tail_sent.at[2], tail_recv.at[2], to).start()
 
-    add_b(1, psum[1])
-    add_b(2, psum[2])
-
-    @pl.when(par == 0)
-    def _():
-        add_b(0, psum[0])
-
-    for j in range(NZ):
-        bpack[j, 0:32] = bsum[j, :, 0:DEPTH]
-        for i in range(4):
-            bpack[j, 32:40, 16 * i : 16 * i + 16] = bsum[j, 8 * i : 8 * i + 8, DEPTH:TOK]
-    for d in far:
+    rows = jnp.concatenate([psum[0], psum[1], psum[2]], axis=1)
+    high = rows.astype(BF16)
+    both = jnp.concatenate([high, (rows - high.astype(F32)).astype(BF16)], axis=0)
+    for d in far + (0,):
         t = (z + d) % NZ
-        remote(bpack.at[t], bs.at[z], tail_sent.at[3], tail_recv.at[3], (dp, t)).start()
-    bs[z] = bpack[z]
+        first = pl.multiple_of(t * TOK, 16)
+        for count, start in ((DEPTH, 0), (TOK - DEPTH, DEPTH)):
+            heads = [attn[s, pl.ds(first + start, count), :] for s in range(3)]
+            found = rows_by_rows(both, jnp.concatenate(heads, axis=1))
+            found = found[0:32] + found[32:64]
+            if start == 0:
+                bpack[t, 0:32] = found
+            else:
+                for i in range(4):
+                    bpack[t, 32:40, 16 * i : 16 * i + 16] = found[8 * i : 8 * i + 8]
+        if d > 0:
+            remote(bpack.at[t], bs.at[z], tail_sent.at[3], tail_recv.at[3], (dp, t)).start()
+        else:
+            bs[z] = bpack[z]
 
     drain(grams.at[0:7], tail_recv.at[2])
     folded = grams[0]
@@ -271,7 +274,7 @@
     work = jnp.where(lane < 32, work, jnp.where(lane - 32 == line, 1.0, 0.0))
     for j in range(32):
         pivot = work[j : j + 1, j : j + 1]
-        scale = 1.0 / jnp.sqrt(pivot)
+        scale = lax.rsqrt(pivot)
         row = work[j : j + 1, :] * scale
         column = jnp.where(line[:, 0:1] > j, work[:, j : j + 1] * scale, 0.0)
         work = jnp.where(line == j, row, work - column * row)
@@ -308,56 +311,55 @@
         cols = slice(wide * j, wide * (j + 1))
         found = part[:, cols] + jnp.dot(a_proj, og[0:DEPTH, cols], preferred_element_type=F32)
         found += jnp.dot(a_rest, og[DEPTH:TOK, cols], preferred_element_type=F32)
-        send[j] = found[0:16].astype(BF16)
-        send[4 + j] = found[16:32].astype(BF16)
-
-    for d in far:
-        t = (z + d) % NZ
-        remote(send.at[t], got.at[z], tail_sent.at[4], tail_recv.at[4], (dp, t)).start()
-    got[z] = send[z]
+        for r in range(2):
+            place = 4 * r + j
+            send[place] = found[16 * r : 16 * r + 16].astype(BF16)
+
+            @pl.when(w == place)
+            def _():
+                got[place] = send[place]
+
+            @pl.when(w != place)
+            def _():
+                to = ((place // 2) * 2 * NY + 2 * y + place % 2, z)
+                remote(send.at[place], got.at[w], tail_sent.at[4], tail_recv.at[4], to).start()
+
+    def summed_over(blocks):
+        total = blocks[0].astype(F32)
+        for j in range(1, 8):
+            total += blocks[j].astype(F32)
+        return total.astype(BF16)
+
     drain(got.at[0:7], tail_recv.at[4])
-    total = got[0].astype(F32)
-    for j in range(1, NZ):
-        total += got[j].astype(F32)
-    cores2[c] = total
-    remote(cores2.at[c], cores2.at[c], tail_sent.at[5], tail_recv.at[5], core_peer).start()
-    drain(cores2.at[0], tail_recv.at[5])
-    xs2[x] = (cores2[0] + cores2[1]).astype(BF16)
-    for to in x_peers:
-        remote(xs2.at[x], xs2.at[x], tail_sent.at[6], tail_recv.at[6], to).start()
-    drain(xs2.at[0:3], tail_recv.at[6])
-    total = xs2[0].astype(F32)
-    for j in range(1, NX):
-        total += xs2[j].astype(F32)
-    ys2[y] = total.astype(BF16)
+    ys2[y] = summed_over(got)
     for to in y_peers:
         remote(ys2.at[y], ys2.at[y], tail_sent.at[7], tail_recv.at[7], to).start()
     drain(ys2.at[0:7], tail_recv.at[7])
-    total = ys2[0].astype(F32)
-    for j in range(1, NY):
-        total += ys2[j].astype(F32)
-    q_out[z] = total.astype(BF16)
+    zs2[z] = summed_over(ys2)
     for to in z_peers:
-        remote(q_out.at[z], q_out.at[z], tail_sent.at[8], tail_recv.at[8], to).start()
+        remote(zs2.at[z], zs2.at[z], tail_sent.at[6], tail_recv.at[6], to).start()
+    drain(zs2.at[0:7], tail_recv.at[6])
+    q_out[w] = summed_over(zs2)
+    for to in w_peers:
+        remote(q_out.at[w], q_out.at[w], tail_sent.at[8], tail_recv.at[8], to).start()
     drain(q_out.at[0:7], tail_recv.at[8])
+
     for s, i in ((1, 2), (2, 0), (2, 1), (2, 2)):
         left(s, i)
 
     @pl.when(par == 0)
     def _():
-        drain(others, step_sent.at[3])
+        drain(others.at[1], step_sent.at[3])
 
     drain(mem.at[0], step_sent.at[4])
-    drain(cores.at[0], step_sent.at[0])
-    drain(xs.at[0:3], step_sent.at[1])
+    drain(xs.at[0:7], step_sent.at[1])
     drain(ys.at[0:7], step_sent.at[2])
     drain(frames.at[0:7], tail_sent.at[0])
     drain(dys.at[0:7], tail_sent.at[1])
     drain(grams.at[0:7], tail_sent.at[2])
     drain(bs.at[0:7], tail_sent.at[3])
     drain(got.at[0:7], tail_sent.at[4])
-    drain(cores2.at[0], tail_sent.at[5])
-    drain(xs2.at[0:3], tail_sent.at[6])
+    drain(zs2.at[0:7], tail_sent.at[6])
     drain(ys2.at[0:7], tail_sent.at[7])
     drain(q_out.at[0:7], tail_sent.at[8])
 
@@ -380,7 +382,8 @@
             vmem((3, 3, SEQ, DEPTH), BF16),
             vmem((2, SEQ, DEPTH), BF16),
             vmem((NZ, 1, TOK), jnp.int32),
-            vmem((NZ, 32, TOK), BF16),
+            vmem((NZ, 48, DEPTH), BF16),
+            vmem((48, DEPTH), F32),
             vmem((SEQ, SEQ), BF16),
             vmem((3, SEQ, DEPTH), BF16),
             vmem((TOK, HD), BF16),
@@ -388,23 +391,20 @@
             vmem((ROWS, HD), BF16),
             vmem((3, 32, DEPTH), F32),
             vmem((3, 32, DEPTH), F32),
-            vmem((2, 3, 32, DEPTH), F32),
             vmem((2, 32, DEPTH), F32),
-            vmem((NX, 3, 32, DEPTH), BF16),
+            vmem((8, 3, 32, DEPTH), BF16),
             vmem((NY, 3, 32, DEPTH), BF16),
             vmem((32, DEPTH), F32),
             vmem((3, 32, DEPTH), F32),
             vmem((32, DEPTH), F32),
             vmem((NZ, 8, DEPTH), F32),
-            vmem((NZ, 32, TOK), F32),
             vmem((NZ, 40, DEPTH), F32),
             vmem((NZ, 40, DEPTH), F32),
             vmem((32, HD), F32),
             vmem((NZ, 16, 640), BF16),
             vmem((NZ, 16, 640), BF16),
-            vmem((2, 16, 640), F32),
-            vmem((NX, 16, 640), BF16),
             vmem((NY, 16, 640), BF16),
+            vmem((NZ, 16, 640), BF16),
             dma((3,)),
             dma((3, 3)),
             dma((3, 3)),

time: 114 us -> 112 us (0.982)
  Pallas kernels: 113 us -> 111 us
    pallas_call x1, Pallas kernels: 112 us -> 109 us  [body(): pl.pallas_call(kernel, out_shape=(jax.ShapeDtypeStruct((32, 384), F32), j...]
where the time goes in v3:
time: 112 us
  Pallas kernels  111 us (99%)
    pallas_call x1, Pallas kernels, body(): pl.pallas_call(kernel, out_shape=(jax.ShapeDtypeStruct((32, 384), F32), j...  109 us

profile of v3, /device:TPU:1, one launch (start us, length us, event | category | flops | bytes accessed | tf_op | source)
XLA Modules:
  0.0 111.8 jit_solution(3439884787103360090)
XLA Ops:
  0.6 109.5 %shard_map.86 = (f32[32,384]{1,0:T(8,128)}, bf16[8,16,640]{2,1,0:T(8,128)(2,1)}) custom-call(bf16[144,2560]{1,0:T(8,128)(2,1)} %bitcast.6, bf16[144,2560]{1,0:T(8,128)(2,1)} %bitcast.7, bf16[144,2560]{1,0:T(8,128)(2,1)} %bitcast.8, s32[1,144]{1,0:T(1,128)} %fr_in.1, bf16[144,2560]{1,0:T(8,128)(2,1)} %bitcast.9, bf16[32,2560]{1,0:T(8,128)(2,1)} %qp_in.1, ...), custom_call_target="tpu_custom_call" | custom-call | tf_op jit(solution)/shard_map/pallas_call | solution.py:376
  110.1 1.7 %shard_map.87 = (f32[32,320]{1,0:T(8,128)}, f32[32,2560]{1,0:T(8,128)}) custom-call(f32[32,384]{1,0:T(8,128)} %get-tuple-element.4.wide_basis, bf16[8,16,640]{2,1,0:T(8,128)(2,1)} %get-tuple-element.5.parts), custom_call_target="tpu_custom_call" | custom-call | tf_op jit(solution)/shard_map/pallas_call | solution.py:420

commit v4 on v3

--- a/solution.py
+++ b/solution.py
@@ -32,7 +32,7 @@
     q_in, k_in, v_in, fr_in, og_in, qp_in, er_in,
     basis, q_out,
     qkv, code, frames, dys, packed, probs, attn, og, qp, er, mem, tok,
-    others, xs, ys, halves, psum, gram, grams, bpack, bs,
+    others, xs, ys, xs1, ys1, halves, psum, gram, grams, bpack, bs,
     part, send, got, ys2, zs2,
     in_sem, recv, sent, step_recv, step_sent, tail_recv, tail_sent,
 ):
@@ -183,6 +183,12 @@
             total += jnp.dot(rest, attn[s, j * TOK + DEPTH : (j + 1) * TOK, :], preferred_element_type=F32)
         tok[s] = total
 
+    def over(blocks):
+        total = blocks[0].astype(F32)
+        for j in range(1, 8):
+            total += blocks[j].astype(F32)
+        return total
+
     def head(s, carry):
         @pl.when(s == 0)
         def _():
@@ -192,9 +198,8 @@
 
         @pl.when(s == 1)
         def _():
-            for i, ahead in enumerate(((2, 1), (2, 2))):
-                left(1, i)
-                send_head(*ahead)
+            left(1, 0)
+            send_head(2, 1)
 
         @pl.when(jnp.logical_or(s > 0, par == 0))
         def _():
@@ -204,35 +209,42 @@
         def _():
             remote(tok.at[0], others.at[1], step_sent.at[3], step_recv.at[3], (dp, mate)).start()
 
+        @pl.when(s == 1)
+        def _():
+            drain(others.at[0], step_recv.at[4])
+
+            @pl.when(par == 1)
+            def _():
+                attn[0] = jnp.zeros((SEQ, DEPTH), BF16)
+                drain(others.at[1], step_recv.at[3])
+                tok[0] = others[1]
+
+            xs[w, 0] = ((mem[0] + others[0]) + tok[0]).astype(BF16)
+            xs[w, 1] = (mem[1] + tok[1]).astype(BF16)
+            for to in w_peers:
+                remote(xs.at[w], xs.at[w], step_sent.at[1], step_recv.at[1], to).start()
+            left(1, 1)
+            send_head(2, 2)
+            drain(xs.at[0:7], step_recv.at[1])
+            ys[y] = over(xs).astype(BF16)
+            for to in y_peers:
+                remote(ys.at[y], ys.at[y], step_sent.at[2], step_recv.at[2], to).start()
+
         return carry
 
     lax.fori_loop(0, 3, head, 0)
 
-    drain(others.at[0], step_recv.at[4])
-
-    @pl.when(par == 1)
-    def _():
-        attn[0] = jnp.zeros((SEQ, DEPTH), BF16)
-        drain(others.at[1], step_recv.at[3])
-        tok[0] = others[1]
-
-    xs[w, 0] = ((mem[0] + others[0]) + tok[0]).astype(BF16)
-    xs[w, 1] = (mem[1] + tok[1]).astype(BF16)
-    xs[w, 2] = (mem[2] + tok[2]).astype(BF16)
+    xs1[w] = (mem[2] + tok[2]).astype(BF16)
     for to in w_peers:
-        remote(xs.at[w], xs.at[w], step_sent.at[1], step_recv.at[1], to).start()
-    drain(xs.at[0:7], step_recv.at[1])
-    total = xs[0].astype(F32)
-    for j in range(1, 8):
-        total += xs[j].astype(F32)
-    ys[y] = total.astype(BF16)
+        remote(xs1.at[w], xs1.at[w], tail_sent.at[5], tail_recv.at[5], to).start()
+    drain(ys.at[0:7], step_recv.at[2])
+    psum[0:2] = over(ys)
+    drain(xs1.at[0:7], tail_recv.at[5])
+    ys1[y] = over(xs1).astype(BF16)
     for to in y_peers:
-        remote(ys.at[y], ys.at[y], step_sent.at[2], step_recv.at[2], to).start()
-    drain(ys.at[0:7], step_recv.at[2])
-    total = ys[0].astype(F32)
-    for j in range(1, NY):
-        total += ys[j].astype(F32)
-    psum[...] = total
+        remote(ys1.at[y], ys1.at[y], step_sent.at[0], step_recv.at[0], to).start()
+    drain(ys1.at[0:7], step_recv.at[0])
+    psum[2] = over(ys1)
 
     own = jnp.where((lane < 64) == even, psum[0], 0.0)
     gram[:, 0:32] = rows_by_rows(own, own, EXACT)
@@ -324,22 +336,16 @@
                 to = ((place // 2) * 2 * NY + 2 * y + place % 2, z)
                 remote(send.at[place], got.at[w], tail_sent.at[4], tail_recv.at[4], to).start()
 
-    def summed_over(blocks):
-        total = blocks[0].astype(F32)
-        for j in range(1, 8):
-            total += blocks[j].astype(F32)
-        return total.astype(BF16)
-
     drain(got.at[0:7], tail_recv.at[4])
-    ys2[y] = summed_over(got)
+    ys2[y] = over(got).astype(BF16)
     for to in y_peers:
         remote(ys2.at[y], ys2.at[y], tail_sent.at[7], tail_recv.at[7], to).start()
     drain(ys2.at[0:7], tail_recv.at[7])
-    zs2[z] = summed_over(ys2)
+    zs2[z] = over(ys2).astype(BF16)
     for to in z_peers:
         remote(zs2.at[z], zs2.at[z], tail_sent.at[6], tail_recv.at[6], to).start()
     drain(zs2.at[0:7], tail_recv.at[6])
-    q_out[w] = summed_over(zs2)
+    q_out[w] = over(zs2).astype(BF16)
     for to in w_peers:
         remote(q_out.at[w], q_out.at[w], tail_sent.at[8], tail_recv.at[8], to).start()
     drain(q_out.at[0:7], tail_recv.at[8])
@@ -352,6 +358,8 @@
         drain(others.at[1], step_sent.at[3])
 
     drain(mem.at[0], step_sent.at[4])
+    drain(xs1.at[0:7], tail_sent.at[5])
+    drain(ys1.at[0:7], step_sent.at[0])
     drain(xs.at[0:7], step_sent.at[1])
     drain(ys.at[0:7], step_sent.at[2])
     drain(frames.at[0:7], tail_sent.at[0])
@@ -392,8 +400,10 @@
             vmem((3, 32, DEPTH), F32),
             vmem((3, 32, DEPTH), F32),
             vmem((2, 32, DEPTH), F32),
-            vmem((8, 3, 32, DEPTH), BF16),
-            vmem((NY, 3, 32, DEPTH), BF16),
+            vmem((8, 2, 32, DEPTH), BF16),
+            vmem((NY, 2, 32, DEPTH), BF16),
+            vmem((8, 32, DEPTH), BF16),
+            vmem((NY, 32, DEPTH), BF16),
             vmem((32, DEPTH), F32),
             vmem((3, 32, DEPTH), F32),
             vmem((32, DEPTH), F32),

time: 112 us -> 109 us (0.973)
  Pallas kernels: 111 us -> 108 us
    pallas_call x1, Pallas kernels: 109 us -> 106 us  [body(): pl.pallas_call(kernel, out_shape=(jax.ShapeDtypeStruct((32, 384), F32), j...]
where the time goes in v4:
time: 109 us
  Pallas kernels  108 us (99%)
    pallas_call x1, Pallas kernels, body(): pl.pallas_call(kernel, out_shape=(jax.ShapeDtypeStruct((32, 384), F32), j...  106 us

profile of v4, /device:TPU:1, one launch (start us, length us, event | category | flops | bytes accessed | tf_op | source)
XLA Modules:
  0.0 108.7 jit_solution(14082483428134768240)
XLA Ops:
  0.6 106.4 %shard_map.86 = (f32[32,384]{1,0:T(8,128)}, bf16[8,16,640]{2,1,0:T(8,128)(2,1)}) custom-call(bf16[144,2560]{1,0:T(8,128)(2,1)} %bitcast.6, bf16[144,2560]{1,0:T(8,128)(2,1)} %bitcast.7, bf16[144,2560]{1,0:T(8,128)(2,1)} %bitcast.8, s32[1,144]{1,0:T(1,128)} %fr_in.1, bf16[144,2560]{1,0:T(8,128)(2,1)} %bitcast.9, bf16[32,2560]{1,0:T(8,128)(2,1)} %qp_in.1, ...), custom_call_target="tpu_custom_call" | custom-call | tf_op jit(solution)/shard_map/pallas_call | solution.py:384
  107.0 1.7 %shard_map.87 = (f32[32,320]{1,0:T(8,128)}, f32[32,2560]{1,0:T(8,128)}) custom-call(f32[32,384]{1,0:T(8,128)} %get-tuple-element.4.wide_basis, bf16[8,16,640]{2,1,0:T(8,128)(2,1)} %get-tuple-element.5.parts), custom_call_target="tpu_custom_call" | custom-call | tf_op jit(solution)/shard_map/pallas_call | solution.py:430

commit v5 on v4

--- a/solution.py
+++ b/solution.py
@@ -33,7 +33,7 @@
     basis, q_out,
     qkv, code, frames, dys, packed, probs, attn, og, qp, er, mem, tok,
     others, xs, ys, xs1, ys1, halves, psum, gram, grams, bpack, bs,
-    part, send, got, ys2, zs2,
+    part, send, got, ys2, zs2, ys3, zs3,
     in_sem, recv, sent, step_recv, step_sent, tail_recv, tail_sent,
 ):
     dp, z = lax.axis_index("dp"), lax.axis_index("ctx")
@@ -337,15 +337,23 @@
                 remote(send.at[place], got.at[w], tail_sent.at[4], tail_recv.at[4], to).start()
 
     drain(got.at[0:7], tail_recv.at[4])
-    ys2[y] = over(got).astype(BF16)
-    for to in y_peers:
-        remote(ys2.at[y], ys2.at[y], tail_sent.at[7], tail_recv.at[7], to).start()
+    total = over(got).astype(BF16)
+    ys2[y] = total[:, 0:384]
+    zs3[z] = total[:, 384:640]
+    for one, two in zip(y_peers, z_peers):
+        remote(ys2.at[y], ys2.at[y], tail_sent.at[7], tail_recv.at[7], one).start()
+        remote(zs3.at[z], zs3.at[z], tail_sent.at[9], tail_recv.at[9], two).start()
     drain(ys2.at[0:7], tail_recv.at[7])
     zs2[z] = over(ys2).astype(BF16)
-    for to in z_peers:
-        remote(zs2.at[z], zs2.at[z], tail_sent.at[6], tail_recv.at[6], to).start()
+    drain(zs3.at[0:7], tail_recv.at[9])
+    ys3[y] = over(zs3).astype(BF16)
+    for one, two in zip(y_peers, z_peers):
+        remote(zs2.at[z], zs2.at[z], tail_sent.at[6], tail_recv.at[6], two).start()
+        remote(ys3.at[y], ys3.at[y], tail_sent.at[10], tail_recv.at[10], one).start()
     drain(zs2.at[0:7], tail_recv.at[6])
-    q_out[w] = over(zs2).astype(BF16)
+    q_out[w, :, 0:384] = over(zs2).astype(BF16)
+    drain(ys3.at[0:7], tail_recv.at[10])
+    q_out[w, :, 384:640] = over(ys3).astype(BF16)
     for to in w_peers:
         remote(q_out.at[w], q_out.at[w], tail_sent.at[8], tail_recv.at[8], to).start()
     drain(q_out.at[0:7], tail_recv.at[8])
@@ -368,6 +376,8 @@
     drain(bs.at[0:7], tail_sent.at[3])
     drain(got.at[0:7], tail_sent.at[4])
     drain(zs2.at[0:7], tail_sent.at[6])
+    drain(zs3.at[0:7], tail_sent.at[9])
+    drain(ys3.at[0:7], tail_sent.at[10])
     drain(ys2.at[0:7], tail_sent.at[7])
     drain(q_out.at[0:7], tail_sent.at[8])
 
@@ -413,15 +423,17 @@
             vmem((32, HD), F32),
             vmem((NZ, 16, 640), BF16),
             vmem((NZ, 16, 640), BF16),
-            vmem((NY, 16, 640), BF16),
-            vmem((NZ, 16, 640), BF16),
+            vmem((NY, 16, 384), BF16),
+            vmem((NZ, 16, 384), BF16),
+            vmem((NY, 16, 256), BF16),
+            vmem((NZ, 16, 256), BF16),
             dma((3,)),
             dma((3, 3)),
             dma((3, 3)),
             dma((6,)),
             dma((6,)),
-            dma((9,)),
-            dma((9,)),
+            dma((11,)),
+            dma((11,)),
         ],
         compiler_params=pltpu.CompilerParams(
             collective_id=0, has_side_effects=True, vmem_limit_bytes=56 * 1024 * 1024

time: 109 us -> 108 us (level)
  no operation moved by 1% of the time
where the time goes in v5:
time: 108 us
  Pallas kernels  107 us (99%)
    pallas_call x1, Pallas kernels, body(): pl.pallas_call(kernel, out_shape=(jax.ShapeDtypeStruct((32, 384), F32), j...  105 us

profile of v5, /device:TPU:1, one launch (start us, length us, event | category | flops | bytes accessed | tf_op | source)
XLA Modules:
  0.0 107.8 jit_solution(17499309993083235022)
XLA Ops:
  0.6 105.5 %shard_map.86 = (f32[32,384]{1,0:T(8,128)}, bf16[8,16,640]{2,1,0:T(8,128)(2,1)}) custom-call(bf16[144,2560]{1,0:T(8,128)(2,1)} %bitcast.6, bf16[144,2560]{1,0:T(8,128)(2,1)} %bitcast.7, bf16[144,2560]{1,0:T(8,128)(2,1)} %bitcast.8, s32[1,144]{1,0:T(1,128)} %fr_in.1, bf16[144,2560]{1,0:T(8,128)(2,1)} %bitcast.9, bf16[32,2560]{1,0:T(8,128)(2,1)} %qp_in.1, ...), custom_call_target="tpu_custom_call" | custom-call | tf_op jit(solution)/shard_map/pallas_call | solution.py:394
  106.1 1.7 %shard_map.87 = (f32[32,320]{1,0:T(8,128)}, f32[32,2560]{1,0:T(8,128)}) custom-call(f32[32,384]{1,0:T(8,128)} %get-tuple-element.4.wide_basis, bf16[8,16,640]{2,1,0:T(8,128)(2,1)} %get-tuple-element.5.parts), custom_call_target="tpu_custom_call" | custom-call | tf_op jit(solution)/shard_map/pallas_call | solution.py:442
